TPU v7x, 128 devices: a whole 4x4x4 slice. The times are simulated.
128 devices in a mesh: layer: 4 (over y_lo, core), shard: 32 (over x, z, y_hi).
Axes of the slice: x: 4, y: 4 (y_hi: 2, y_lo: 2; y = y_hi * 2 + y_lo), z: 4, core: 2. Of those that a mesh axis runs over, the one named last changes fastest.
Arguments:
- layer_inputs: bfloat16 [4, 1536, 5120], P('layer', 'shard'), may hold values from -6 to 6
- output_grads: bfloat16 [4, 1536, 16384], P('layer', 'shard'), may hold values from -6 to 6
- input_basis: bfloat16 [4, 10, 512, 512], P('layer'), may hold values from -0.25 to 0.25
- grad_basis: bfloat16 [4, 32, 512, 512], P('layer', 'shard'), may hold values from -0.25 to 0.25
- eigenvalues: float32 [4, 16384, 5120], P('layer', 'shard'), may hold values from 0.1 to 10
- layer_table: int32 [4], replicated, may hold values from 0 to 3, each once
- batch_ids: int32 [16], replicated, may hold values from 0 to 3
Outputs:
- scores: float32 [16, 16], replicated
- batch_scores: float32 [16, 4], replicated
- layer_totals: float32 [4, 16], replicated
All inputs are finite; a program needn't handle non-finite values.
Results may differ from a plain program's by a relative error of at most 0.0063.
Values may be sent and summed in bfloat16 or wider, within the bound.
A program may use at most 384 MiB of HBM per device.

v0:
```python
import math

import jax
import jax.numpy as jnp
from jax import lax
from jax.sharding import PartitionSpec as P

NQ = 16
SQ = 32
NT = 16
ST = 64
NB = 4


DAMPING = 0.1


def project_layers(row_block, bases):
    layers, row_count, model_width = row_block.shape
    block_count = bases.shape[1]
    block_width = bases.shape[2]
    blocked = row_block.reshape(layers, row_count, block_count, block_width)
    product = jnp.einsum("lrkc,lkcd->lrkd", blocked, bases, preferred_element_type=jnp.float32)
    return product.reshape(layers, row_count, model_width).astype(jnp.bfloat16)


def per_device(
    layer_inputs, output_grads, input_basis, grad_basis, eigenvalues, layer_table, batch_ids
):
    input_proj = project_layers(
        lax.all_gather(layer_inputs, "shard", axis=1, tiled=True), input_basis
    )
    columns = lax.all_to_all(output_grads, "shard", split_axis=2, concat_axis=1, tiled=True)
    local_layers = layer_inputs.shape[0]
    model_width = layer_inputs.shape[2]
    block_width = grad_basis.shape[2]
    total_layers = layer_table.shape[0]
    shard_count = lax.axis_size("shard")
    norm_factor = 1.0 / math.sqrt(block_width * shard_count * model_width * SQ * ST)
    query_rows = NQ * SQ
    stride_rows = min(128, block_width)
    first_slot = lax.axis_index("layer") * local_layers
    grad_proj = jnp.dot(columns[0], grad_basis[0, 0], preferred_element_type=jnp.float32).astype(
        jnp.bfloat16
    )
    inverse = 1.0 / (eigenvalues[0] + DAMPING)
    query_in = input_proj[0, :query_rows].reshape(NQ, SQ, model_width)
    train_in = input_proj[0, query_rows:].reshape(NT, ST, model_width)
    query_out = grad_proj[:query_rows].reshape(NQ, SQ, block_width)
    train_out = grad_proj[query_rows:].reshape(NT, ST, block_width)
    partial_value = jnp.zeros((NQ, NT), jnp.float32)
    for offset in range(0, block_width, stride_rows):
        query_grad = jnp.einsum(
            "qsi,qsj->qij",
            query_out[:, :, offset : offset + stride_rows],
            query_in,
            preferred_element_type=jnp.float32,
        )
        weighted = (query_grad * inverse[None, offset : offset + stride_rows]).astype(jnp.bfloat16)
        train_grad = jnp.einsum(
            "tsi,tsj->tij",
            train_out[:, :, offset : offset + stride_rows],
            train_in,
            preferred_element_type=jnp.float32,
        ).astype(jnp.bfloat16)
        partial_value = partial_value + jnp.einsum(
            "qij,tij->qt", weighted, train_grad, preferred_element_type=jnp.float32
        )
    partial_value = partial_value * norm_factor
    model_layer = lax.dynamic_index_in_dim(layer_table, first_slot + 0, 0, keepdims=False)
    layer_marker = (jnp.arange(total_layers, dtype=jnp.int32) == model_layer).astype(jnp.float32)
    totals_part = layer_marker[:, None] * jnp.sum(partial_value, axis=1)[None, :]
    scores, layer_totals = lax.psum((partial_value, totals_part), ("layer", "shard"))
    batch_marks = (batch_ids[:, None] == jnp.arange(NB, dtype=jnp.int32)[None, :]).astype(
        jnp.float32
    )
    batch_scores = jnp.sum(scores[:, :, None] * batch_marks[None, :, :], axis=1)
    return (scores, batch_scores, layer_totals)


def solution(mesh):
    in_specs = (
        P("layer", "shard", None),
        P("layer", "shard", None),
        P("layer", None, None, None),
        P("layer", "shard", None, None),
        P("layer", "shard", None),
        P(),
        P(),
    )
    out_specs = (P(), P(), P())
    return jax.shard_map(
        per_device, mesh=mesh, in_specs=in_specs, out_specs=out_specs, check_vma=False
    )
```

profile of v0, /device:TPU:1, one launch (start us, length us, event | category | flops | bytes accessed | tf_op | source)
XLA Modules:
  0.0 785.4 jit_solution(13081103606337360496)
XLA Ops:
  7.9 16.5 %copy.54 = bf16[1,48,16384]{1,0,2:T(2,128)(2,1)} copy(bf16[1,48,16384]{2,1,0:T(8,128)(2,1)} %param.8) | data formatting | bytes 3145728 | tf_op args[1]
  24.9 90.9 %reduce = bf16[16384,48]{1,0:T(8,128)(2,1)} reduce(bf16[16384,1,48]{2,1,0:T(2,128)(2,1)} %bitcast.70, bf16[]{:T(256)} %broadcast.24), dimensions={1}, to_apply=%bitcast.49.reduce_sub_computation | reduce | bytes 3145730
  115.8 10.0 %reshape.83 = bf16[32,2,12288]{2,1,0:T(2,128)(2,1)} reshape(bf16[16384,48]{1,0:T(8,128)(2,1)} %reduce) | data formatting | bytes 3145728
  125.8 11.7 %all-to-all-start = ((bf16[32,2,12288]{2,1,0:T(2,128)(2,1)}), bf16[32,2,12288]{2,1,0:T(2,128)(2,1)}, u32[]{:S(2)}, u32[]{:S(2)}) async-start(bf16[32,2,12288]{2,1,0:T(2,128)(2,1)} %reshape.83), calls=%async_computation | async-start | bytes 3145728 | tf_op jit(solution)/shard_map/all_to_all | solution.py:33
  138.6 5.3 add_divide_fusion
  144.0 1.2 compare_convert_fusion
  145.1 3.3 slice_bitcast_fusion
  148.4 13.4 %all-to-all-done = bf16[32,2,12288]{2,1,0:T(2,128)(2,1)} async-done(((bf16[32,2,12288]{2,1,0:T(2,128)(2,1)}), bf16[32,2,12288]{2,1,0:T(2,128)(2,1)}, u32[]{:S(2)}, u32[]{:S(2)}) %all-to-all-start) | async-done | bytes 1572896 | tf_op jit(solution)/shard_map/all_to_all | solution.py:33
  161.8 19.8 %reshape.84 = bf16[16384,1,48]{2,1,0:T(2,128)(2,1)} reshape(bf16[32,2,12288]{2,1,0:T(2,128)(2,1)} %all-to-all-done) | data formatting | bytes 3145728
  181.7 16.4 %copy.55 = bf16[1,48,16384]{2,1,0:T(8,128)(2,1)} copy(bf16[1,48,16384]{1,0,2:T(2,128)(2,1)} %bitcast.71) | data formatting | bytes 3145728 | tf_op jit(solution)/shard_map/all_to_all | solution.py:33
  198.1 2.0 copy.76
  201.1 1.0 convolution_convert_fusion.5
  202.1 1.0 slice.84
  203.2 20.6 %copy.57 = bf16[1,1536,5120]{1,2,0:T(8,128)(2,1)} copy(bf16[1,1536,5120]{2,1,0:T(8,128)(2,1)} %all-gather.2.cloned.1.call-done) | data formatting | bytes 31457280 | tf_op jit(solution)/shard_map/all_gather | solution.py:31
  223.8 18.0 %convolution_convert_fusion = bf16[10,512,1536]{2,1,0:T(8,128)(2,1)} fusion(bf16[1536,10,512]{0,2,1:T(8,128)(2,1)} %bitcast.74, bf16[1,10,512,512]{3,2,1,0:T(8,128)(2,1)} %param.9), kind=kOutput, calls=%fused_computation.16 | convolution fusion | flops 8060928000 | bytes 36700160 | tf_op jit(solution)/shard_map/lrkc,lkcd->lrkd/dot_general | solution.py:23
  241.8 5.3 slice.82
  247.1 9.2 %slice.86 = bf16[1,1024,5120]{1,2,0:T(8,128)(2,1)} slice(bf16[1,1536,5120]{1,2,0:T(8,128)(2,1)} %bitcast.73), slice={[0:1], [512:1536], [0:5120]} | slice | bytes 20971520 | tf_op jit(solution)/shard_map/slice | solution.py:48
  256.2 13.8 %copy.75 = bf16[1,1024,5120]{2,1,0:T(8,128)(2,1)} copy(bf16[1,1024,5120]{1,2,0:T(8,128)(2,1)} %slice.86) | data formatting | bytes 20971520
  270.0 12.8 %convolution_convert_fusion.4 = bf16[16,128,5120]{2,1,0:T(8,128)(2,1)} fusion(bf16[16,64,5120]{2,1,0:T(8,128)(2,1)} %bitcast.62, bf16[16,64,512]{2,1,0:T(8,128)(2,1)} %bitcast.77), kind=kOutput, calls=%fused_computation.20 | convolution fusion | flops 1352663040 | bytes 31719424 | tf_op jit(solution)/shard_map/tsi,tsj->tij/dot_general | solution.py:60
  282.8 12.6 %convolution_convert_fusion.3 = bf16[16,128,5120]{2,1,0:T(8,128)(2,1)} fusion(bf16[16,64,5120]{2,1,0:T(8,128)(2,1)} %bitcast.63, bf16[16,64,512]{2,1,0:T(8,128)(2,1)} %bitcast.78), kind=kOutput, calls=%fused_computation.19 | convolution fusion | flops 1352663040 | bytes 31719424 | tf_op jit(solution)/shard_map/tsi,tsj->tij/dot_general | solution.py:60
  295.3 12.6 %convolution_convert_fusion.2 = bf16[16,128,5120]{2,1,0:T(8,128)(2,1)} fusion(bf16[16,64,5120]{2,1,0:T(8,128)(2,1)} %bitcast.64, bf16[16,64,512]{2,1,0:T(8,128)(2,1)} %bitcast.79), kind=kOutput, calls=%fused_computation.18 | convolution fusion | flops 1352663040 | bytes 31719424 | tf_op jit(solution)/shard_map/tsi,tsj->tij/dot_general | solution.py:60
  307.9 12.6 %convolution_convert_fusion.1 = bf16[16,128,5120]{2,1,0:T(8,128)(2,1)} fusion(bf16[16,64,5120]{2,1,0:T(8,128)(2,1)} %bitcast.65, bf16[16,64,512]{2,1,0:T(8,128)(2,1)} %bitcast.80), kind=kOutput, calls=%fused_computation.17 | convolution fusion | flops 1352663040 | bytes 31719424 | tf_op jit(solution)/shard_map/tsi,tsj->tij/dot_general | solution.py:60
  320.5 8.0 %copy.74 = bf16[1,512,5120]{2,1,0:T(8,128)(2,1)} copy(bf16[1,512,5120]{1,2,0:T(8,128)(2,1)} %slice.82) | data formatting | bytes 10485760
  328.5 12.5 %multiply_convert_fusion.3 = bf16[16,128,5120]{2,1,0:T(8,128)(2,1)} fusion(f32[128,5120]{1,0:T(8,128)} %get-tuple-element.23, bf16[16,32,5120]{2,1,0:T(8,128)(2,1)} %bitcast.66, bf16[16,32,512]{2,1,0:T(8,128)(2,1)S(1)} %bitcast.81), kind=kOutput, calls=%fused_computation.3 | convolution fusion | flops 692060160 | bytes 28966912 | tf_op jit(solution)/shard_map/qsi,qsj->qij/dot_general | solution.py:53
  341.0 12.1 %multiply_convert_fusion.2 = bf16[16,128,5120]{2,1,0:T(8,128)(2,1)} fusion(f32[128,5120]{1,0:T(8,128)} %get-tuple-element.22, bf16[16,32,5120]{2,1,0:T(8,128)(2,1)} %bitcast.67, bf16[16,32,512]{2,1,0:T(8,128)(2,1)S(1)} %bitcast.82), kind=kOutput, calls=%fused_computation.2 | convolution fusion | flops 692060160 | bytes 28966912 | tf_op jit(solution)/shard_map/qsi,qsj->qij/dot_general | solution.py:53
  353.2 12.2 %multiply_convert_fusion.1 = bf16[16,128,5120]{2,1,0:T(8,128)(2,1)} fusion(f32[128,5120]{1,0:T(8,128)} %get-tuple-element.21, bf16[16,32,5120]{2,1,0:T(8,128)(2,1)} %bitcast.68, bf16[16,32,512]{2,1,0:T(8,128)(2,1)S(1)} %bitcast.83), kind=kOutput, calls=%fused_computation.1 | convolution fusion | flops 692060160 | bytes 28966912 | tf_op jit(solution)/shard_map/qsi,qsj->qij/dot_general | solution.py:53
  365.4 11.6 %multiply_convert_fusion = bf16[16,128,5120]{2,1,0:T(8,128)(2,1)} fusion(f32[128,5120]{1,0:T(8,128)S(1)} %get-tuple-element.20, bf16[16,32,5120]{2,1,0:T(8,128)(2,1)} %bitcast.69, bf16[16,32,512]{2,1,0:T(8,128)(2,1)S(1)} %bitcast.84), kind=kOutput, calls=%fused_computation | convolution fusion | flops 692060160 | bytes 28966912 | tf_op jit(solution)/shard_map/qsi,qsj->qij/dot_general | solution.py:53
  377.0 88.2 %fusion.13 = f32[16,16]{0,1:T(8,128)S(1)} fusion(bf16[16,128,5120]{2,1,0:T(8,128)(2,1)} %convolution_convert_fusion.4, bf16[16,128,5120]{2,1,0:T(8,128)(2,1)} %multiply_convert_fusion.3), kind=kOutput, calls=%fused_computation.29 | convolution fusion | flops 335544320 | bytes 41944064 | tf_op jit(solution)/shard_map/qij,tij->qt/dot_general | solution.py:66
  465.3 87.0 %fusion.43 = f32[16,16]{0,1:T(8,128)S(1)} fusion(f32[16,16]{0,1:T(8,128)S(1)} %fusion.13, bf16[16,128,5120]{2,1,0:T(8,128)(2,1)} %convolution_convert_fusion.3, bf16[16,128,5120]{2,1,0:T(8,128)(2,1)} %multiply_convert_fusion.2), kind=kOutput, calls=%fused_computation.35 | convolution fusion | flops 335544576 | bytes 41945088 | tf_op jit(solution)/shard_map/qij,tij->qt/dot_general | solution.py:66
  552.3 87.6 %fusion.38 = f32[16,16]{0,1:T(8,128)S(1)} fusion(f32[16,16]{0,1:T(8,128)S(1)} %fusion.43, bf16[16,128,5120]{2,1,0:T(8,128)(2,1)} %convolution_convert_fusion.2, bf16[16,128,5120]{2,1,0:T(8,128)(2,1)} %multiply_convert_fusion.1), kind=kOutput, calls=%fused_computation.34 | convolution fusion | flops 335544576 | bytes 41945088 | tf_op jit(solution)/shard_map/qij,tij->qt/dot_general | solution.py:66
  639.9 71.2 %fusion.63 = (f32[16]{0:T(128)S(1)}, f32[16,16]{0,1:T(8,128)S(1)}) fusion(f32[16,16]{0,1:T(8,128)S(1)} %fusion.38, bf16[16,128,5120]{2,1,0:T(8,128)(2,1)} %convolution_convert_fusion.1, bf16[16,128,5120]{2,1,0:T(8,128)(2,1)} %multiply_convert_fusion), kind=kOutput, calls=%fused_computation.51 | convolution fusion | flops 335545088 | bytes 41945152 | tf_op jit(solution)/shard_map/qij,tij->qt/dot_general | solution.py:66
  711.2 66.5 %all-reduce = (f32[16,16]{0,1:T(8,128)S(1)}, f32[4,16]{1,0:T(4,128)}) all-reduce(f32[16,16]{0,1:T(8,128)S(1)} %get-tuple-element.25, f32[4,16]{1,0:T(4,128)S(1)} %broadcast_multiply_fusion), channel_id=1, replica_groups=mesh['layer'=4,'shard'=32] {'layer','shard'}, use_global_device_ids=true, to_apply=%region_0.1 | all-reduce | flops 320 | bytes 2560 | tf_op jit(solution)/shard_map/psum | solution.py:73
  (26 shorter events, 4.3 us)
Async XLA Ops:
  7.2 193.9 %copy-start = (bf16[1,1,512,512]{3,2,1,0:T(8,128)(2,1)S(1)}, bf16[1,1,512,512]{3,2,1,0:T(8,128)(2,1)}, u32[]{:S(2)}) copy-start(bf16[1,1,512,512]{3,2,1,0:T(8,128)(2,1)} %param.10) | copy-start | bytes 1572868
  7.2 196.0 %all-gather.2.cloned.1.call-start = ((), (), s32[]{:S(2)}) async-start(), calls=%async_computation.1 | async-start | bytes 16220160 | tf_op jit(solution)/shard_map/all_gather | solution.py:31
  7.9 129.5 %copy-start.6 = (s32[4]{0:T(128)S(1)}, s32[4]{0:T(128)}, u32[]{:S(2)}) copy-start(s32[4]{0:T(128)} %param.12) | copy-start | bytes 52
  7.9 130.1 %copy-start.4 = (s32[16]{0:T(128)S(1)}, s32[16]{0:T(128)}, u32[]{:S(2)}) copy-start(s32[16]{0:T(128)} %param.13) | copy-start | bytes 196
  125.8 36.1 %all-to-all-start = ((bf16[32,2,12288]{2,1,0:T(2,128)(2,1)}), bf16[32,2,12288]{2,1,0:T(2,128)(2,1)}, u32[]{:S(2)}, u32[]{:S(2)}) async-start(bf16[32,2,12288]{2,1,0:T(2,128)(2,1)} %reshape.83), calls=%async_computation | async-start | bytes 3145728 | tf_op jit(solution)/shard_map/all_to_all | solution.py:33
  552.3 226.1 %copy-start.1 = (bf16[1,1,512,512]{3,2,1,0:T(8,128)(2,1)S(1)}, bf16[1,1,512,512]{3,2,1,0:T(8,128)(2,1)}, u32[]{:S(2)}) copy-start(bf16[1,1,512,512]{3,2,1,0:T(8,128)(2,1)} %param.10) | copy-start | bytes 1572868
  639.9 71.2 %copy-start.5 = (f32[4]{0:T(128)S(1)}, f32[4]{0:T(128)}, u32[]{:S(2)}) copy-start(f32[4]{0:T(128)} %compare_convert_fusion) | copy-start | bytes 52
  639.9 137.8 %copy-start.3 = (f32[16,4]{0,1:T(4,128)S(1)}, f32[16,4]{0,1:T(4,128)}, u32[]{:S(2)}) copy-start(f32[16,4]{0,1:T(4,128)} %fusion.62) | copy-start | bytes 772
  777.7 0.7 copy-start.2
Sparse Core Ops, SparseCore 0:
  11.0 166.6 all-gather.1
where the time goes:
time: 796 us; the launch traced here: 785 us
  matrix products  452 us (57%)
  local copies, waits for them, and re-layouts  128 us (16%)
  other arithmetic  98.7 us (12%)
  blocking collectives  66.5 us (8%)
  between operations  14.4 us (2%)
  waiting for transfers between devices  14.1 us (2%)
  starting transfers between devices  11.7 us (1%)
    dot_general x4, matrix products, per_device(): jnp.einsum('qij,tij->qt', weighted, train_grad, preferred_element_type=jn...  334 us
    unnamed x1, other arithmetic  90.9 us
    unnamed x22, local copies, waits for them, and re-layouts  70.6 us
    psum x1, blocking collectives, per_device(): lax.psum((partial_value, totals_part), ('layer', 'shard'))  66.5 us
    dot_general x4, matrix products, per_device(): jnp.einsum('tsi,tsj->tij', train_out[:, :, offset:offset + stride_rows],...  50.5 us
    dot_general x4, matrix products, per_device(): jnp.einsum('qsi,qsj->qij', query_out[:, :, offset:offset + stride_rows],...  48.5 us
    all_gather x1, local copies, waits for them, and re-layouts, per_device(): lax.all_gather(layer_inputs, 'shard', axis=1, tiled=True)  20.6 us
    dot_general x1, matrix products, project_layers(): jnp.einsum('lrkc,lkcd->lrkd', blocked, bases, preferred_element_type=jnp....  18 us
  transfers between devices with their start and end apart: 2, of which 1 were waited for; matrix products, arithmetic and copies ran while one was open for 22% of the time, Pallas kernels for 0%

commit v1 on v0

v1 whole, which is shorter than its diff:
```python
import functools
import math

import jax
import jax.numpy as jnp
from jax import lax
from jax.experimental import pallas as pl
from jax.experimental.pallas import tpu as pltpu
from jax.sharding import PartitionSpec as P

NQ = 16
SQ = 32
NT = 16
ST = 64
NB = 4
DAMPING = 0.1

D = 5120
BLK = 512
CHUNKS = D // BLK
HALF = BLK // 2
SHARDS = 32
LAYERS = 4
ROWS = 48
QTOK = NQ * SQ
GROUP = 4
LEAD = 4
MESH = pl.DeviceIdType.MESH
F32 = jnp.float32
BF = jnp.bfloat16


def where_am_i():
    shard = lax.axis_index("shard")
    return {"x": shard // 8, "z": (shard // 2) % 4, "h": shard % 2}


def shifted(at, axis, step):
    out = dict(at)
    out[axis] = (at[axis] + step + 4) % (2 if axis == "h" else 4)
    return out


def device_of(at):
    return (lax.axis_index("layer"), (at["x"] * 4 + at["z"]) * 2 + at["h"])


def region(buf, c, near, far, at, msg):
    def block(first, second, rows):
        ix = {near: first, far: second}
        return buf.at[c, ix["x"], ix["z"], rows]

    low, high, whole = pl.ds(0, ROWS), pl.ds(ROWS, ROWS), pl.ds(0, 2 * ROWS)
    if msg == 0:
        return block(at[near], at[far], pl.ds(pl.multiple_of(at["h"] * ROWS, 16), ROWS))
    if msg in (1, 2):
        return block(at[near], at[far], whole)
    if msg == 3:
        return block(shifted(at, near, -1)[near], at[far], low)
    if msg == 4:
        return block(shifted(at, near, 1)[near], at[far], high)
    if msg in (5, 6):
        return block(pl.ds(0, 4), at[far], whole)
    if msg == 7:
        return block(pl.ds(0, 2), shifted(at, far, -1)[far], whole)
    return block(pl.ds(2, 2), shifted(at, far, 1)[far], whole)


def moves(near, far):
    return (("h", 1), (near, 1), (near, -1), (near, 1), (near, -1), (far, 1), (far, -1), (far, 1), (far, -1))


STAGES = ((0,), (1, 2), (3, 4), (5, 6), (7, 8))


def kernel(
    x_ref, og_ref, ib_ref, gb_ref, eg_ref, out_ref,
    ga, gb2, go, ib, gbt, tot, qot, ev, inv, q, ti, v, r, part, lpart,
    ib_sem, ev_sem, own_sem, a_send, a_recv, ga_send, ga_recv, gb_send, gb_recv, r_send, r_recv, l_send, l_recv,
):
    me = lax.axis_index("shard")
    layer = lax.axis_index("layer")
    at = where_am_i()
    halves = (
        (ga, ga_send, ga_recv, "x", "z"),
        (gb2, gb_send, gb_recv, "z", "x"),
    )

    def basis_copy(c):
        return pltpu.make_async_copy(ib_ref.at[c], ib.at[c], ib_sem.at[c])

    def eig_copy(c, slot):
        cols = pl.ds(pl.multiple_of(c * BLK, BLK), BLK)
        return pltpu.make_async_copy(eg_ref.at[:, cols], ev.at[slot], ev_sem.at[slot])

    for c in range(CHUNKS):
        basis_copy(c).start()
    eig_copy(0, 0).start()

    bar = pltpu.get_barrier_semaphore()

    def greet(i, _):
        pl.semaphore_signal(bar, inc=1, device_id=(layer, (me + i) % SHARDS), device_id_type=MESH)
        return 0

    lax.fori_loop(1, SHARDS, greet, 0)
    for i in range(1, LAYERS):
        pl.semaphore_signal(bar, inc=1, device_id=((layer + i) % LAYERS, me), device_id_type=MESH)
    pl.semaphore_wait(bar, SHARDS - 1 + LAYERS - 1)

    def rows_of(s):
        return pl.ds(pl.multiple_of(s * ROWS, 16), ROWS)

    def cols_of(s):
        return pl.ds(pl.multiple_of(s * BLK, BLK), BLK)

    def column_send(i):
        to = (me + i) % SHARDS
        return pltpu.make_async_remote_copy(
            src_ref=og_ref.at[:, cols_of(to)], dst_ref=go.at[rows_of(me)],
            send_sem=a_send.at[i], recv_sem=a_recv.at[i], device_id=(layer, to), device_id_type=MESH,
        )

    def column_recv(i):
        frm = (me + SHARDS - i) % SHARDS
        return pltpu.make_async_remote_copy(
            src_ref=og_ref.at[:, cols_of(me)], dst_ref=go.at[rows_of(frm)],
            send_sem=a_send.at[i], recv_sem=a_recv.at[i], device_id=(layer, frm), device_id_type=MESH,
        )

    own = pltpu.make_async_copy(og_ref.at[:, cols_of(me)], go.at[rows_of(me)], own_sem)
    own.start()

    def message(half, c, msg, receive):
        buf, send, recv, near, far = halves[half]
        axis, step = moves(near, far)[msg]
        sender = shifted(at, axis, -step) if receive else at
        piece = region(buf, c, near, far, sender, msg)
        return pltpu.make_async_remote_copy(
            src_ref=piece, dst_ref=piece, send_sem=send.at[c, msg], recv_sem=recv.at[c, msg],
            device_id=device_of(shifted(at, axis, step)), device_id_type=MESH,
        )

    def stage(half, number, c):
        def go_on():
            if number > 0:
                for msg in STAGES[number - 1]:
                    message(half, c, msg, True).wait_recv()
            if number < len(STAGES):
                for msg in STAGES[number]:
                    message(half, c, msg, False).start()

        return go_on

    def step_half(half, k):
        for number, lag in ((4, -3), (3, -2), (2, -1), (1, 0), (0, 2)):
            c = k + lag
            pl.when(jnp.logical_and(c >= 0, c < CHUNKS))(stage(half, number, c))

    def project(c, _):
        basis_copy(c).wait()
        mine = jnp.dot(x_ref[:, cols_of(c)], ib[c], preferred_element_type=F32).astype(BF)
        here = pl.ds(pl.multiple_of(at["h"] * ROWS, 16), ROWS)
        ga[c, at["x"], at["z"], here, :] = mine[:, :HALF]
        gb2[c, at["x"], at["z"], here, :] = mine[:, HALF:]

        @pl.when(c < 2)
        def _():
            for half in range(2):
                message(half, c, 0, False).start()

        return 0

    lax.fori_loop(0, 2, project, 0)

    def send_columns(i, _):
        column_send(i).start()
        return 0

    lax.fori_loop(1, SHARDS, send_columns, 0)
    lax.fori_loop(2, CHUNKS, project, 0)
    gbt[...] = gb_ref[...].T
    r[...] = jnp.zeros_like(r)

    def fill(k, _):
        step_half(0, k)
        step_half(1, k)
        return 0

    lax.fori_loop(0, LEAD, fill, 0)

    own.wait()

    def take_columns(i, _):
        column_recv(i).wait_recv()
        return 0

    lax.fori_loop(1, SHARDS, take_columns, 0)

    def turned(rows):
        return lax.dot_general(
            gbt[...], go[rows, :], (((1,), (1,)), ((), ())), preferred_element_type=F32
        ).astype(BF)

    qot[...] = turned(pl.ds(0, QTOK)).astype(F32)

    def turn_train(t, _):
        tot[t] = turned(pl.ds(pl.multiple_of(QTOK + t * ST, ST), ST))
        return 0

    lax.fori_loop(0, NT, turn_train, 0)

    def compute(k):
        c = k - LEAD
        slot = c % 2
        for half in range(2):
            for msg in STAGES[4]:
                message(half, c, msg, True).wait_recv()
        eig_copy(c, slot).wait()

        @pl.when(c + 1 < CHUNKS)
        def _():
            eig_copy(c + 1, 1 - slot).start()

        inv[...] = 1.0 / (ev[slot] + DAMPING)
        for half, buf in enumerate((ga, gb2)):
            cols = slice(half * HALF, half * HALF + HALF)
            q[0:384, cols] = buf[c, 0].reshape(384, HALF)
            q[384:480, cols] = buf[c, 1, 0]
            q[480:512, cols] = buf[c, 1, 1, 0:32]
            ti[0:64, cols] = buf[c, 1, 1, 32:96]
            ti[64:160, cols] = buf[c, 1, 2]
            ti[160:256, cols] = buf[c, 1, 3]
            ti[256:640, cols] = buf[c, 2].reshape(384, HALF)
            ti[640:1024, cols] = buf[c, 3].reshape(384, HALF)

        def group(g, _):
            @pl.when(g == 2)
            def _():
                step_half(1, k)

            for n in range(GROUP):
                t = g * GROUP + n
                grad = jnp.dot(tot[t], ti[pl.ds(pl.multiple_of(t * ST, ST), ST), :], preferred_element_type=F32)
                v[n * BLK : (n + 1) * BLK, :] = (grad * inv[...]).astype(BF)
            for o in range(0, QTOK, 256):
                z = lax.dot_general(
                    v[...], q[o : o + 256, :], (((1,), (1,)), ((), ())), preferred_element_type=F32
                )
                for n in range(GROUP):
                    t = g * GROUP + n
                    r[pl.ds(t, 1), o : o + 256] += jnp.sum(
                        z[n * BLK : (n + 1) * BLK] * qot[:, o : o + 256], axis=0, keepdims=True
                    )
            return 0

        lax.fori_loop(0, NT // GROUP, group, 0)

    def main(k, _):
        step_half(0, k)
        compute(k)
        return 0

    lax.fori_loop(LEAD, CHUNKS + LEAD, main, 0)

    token = lax.broadcasted_iota(jnp.int32, (QTOK, 128), 0) // SQ
    query = lax.broadcasted_iota(jnp.int32, (QTOK, 128), 1)
    marks = (token == query).astype(F32)
    norm_factor = 1.0 / math.sqrt(BLK * SHARDS * D * SQ * ST)
    part[me] = norm_factor * jnp.dot(r[...], marks, preferred_element_type=F32, precision=lax.Precision.HIGHEST)

    def part_copy(i, receive):
        to = (me + i) % SHARDS
        slot = (me + SHARDS - i) % SHARDS if receive else me
        return pltpu.make_async_remote_copy(
            src_ref=part.at[slot], dst_ref=part.at[slot], send_sem=r_send.at[i], recv_sem=r_recv.at[i],
            device_id=(layer, to), device_id_type=MESH,
        )

    def layer_copy(i, receive):
        to = (layer + i) % LAYERS
        slot = (layer + LAYERS - i) % LAYERS if receive else layer
        return pltpu.make_async_remote_copy(
            src_ref=lpart.at[slot], dst_ref=lpart.at[slot], send_sem=l_send.at[i], recv_sem=l_recv.at[i],
            device_id=(to, me), device_id_type=MESH,
        )

    def part_start(i, _):
        part_copy(i, False).start()
        return 0

    def part_take(i, _):
        part_copy(i, True).wait_recv()
        return 0

    lax.fori_loop(1, SHARDS, part_start, 0)
    lax.fori_loop(1, SHARDS, part_take, 0)
    lpart[layer] = jnp.sum(part[...], axis=0)
    for i in range(1, LAYERS):
        layer_copy(i, False).start()
    for i in range(1, LAYERS):
        layer_copy(i, True).wait_recv()
    out_ref[...] = lpart[...]

    def sent(i, _):
        column_send(i).wait_send()
        part_copy(i, False).wait_send()
        return 0

    lax.fori_loop(1, SHARDS, sent, 0)
    for i in range(1, LAYERS):
        layer_copy(i, False).wait_send()

    def chunk_sent(c, _):
        for half in range(2):
            for msg in range(9):
                message(half, c, msg, False).wait_send()
        return 0

    lax.fori_loop(0, CHUNKS, chunk_sent, 0)


def layer_parts(layer_inputs, output_grads, input_basis, grad_basis, eigenvalues):
    vmem = pl.BlockSpec(memory_space=pltpu.VMEM)
    hbm = pl.BlockSpec(memory_space=pl.ANY)
    dma = pltpu.SemaphoreType.DMA
    scratch = [
        pltpu.VMEM((CHUNKS, 4, 4, 2 * ROWS, HALF), BF),
        pltpu.VMEM((CHUNKS, 4, 4, 2 * ROWS, HALF), BF),
        pltpu.VMEM((SHARDS * ROWS, BLK), BF),
        pltpu.VMEM((CHUNKS, BLK, BLK), BF),
        pltpu.VMEM((BLK, BLK), BF),
        pltpu.VMEM((NT, BLK, ST), BF),
        pltpu.VMEM((BLK, QTOK), F32),
        pltpu.VMEM((2, BLK, BLK), F32),
        pltpu.VMEM((BLK, BLK), F32),
        pltpu.VMEM((QTOK, BLK), BF),
        pltpu.VMEM((NT * ST, BLK), BF),
        pltpu.VMEM((GROUP * BLK, BLK), BF),
        pltpu.VMEM((NT, QTOK), F32),
        pltpu.VMEM((SHARDS, NT, 128), F32),
        pltpu.VMEM((LAYERS, NT, 128), F32),
        dma((CHUNKS,)), dma((2,)), dma,
        dma((SHARDS,)), dma((SHARDS,)),
        dma((CHUNKS, 9)), dma((CHUNKS, 9)), dma((CHUNKS, 9)), dma((CHUNKS, 9)),
        dma((SHARDS,)), dma((SHARDS,)),
        dma((LAYERS,)), dma((LAYERS,)),
    ]
    return pl.pallas_call(
        kernel,
        out_shape=jax.ShapeDtypeStruct((LAYERS, NT, 128), F32),
        in_specs=[vmem, hbm, hbm, vmem, hbm],
        out_specs=vmem,
        scratch_shapes=scratch,
        compiler_params=pltpu.CompilerParams(
            collective_id=0, has_side_effects=True, vmem_limit_bytes=56 * 2**20
        ),
    )(layer_inputs, output_grads, input_basis, grad_basis, eigenvalues)


def per_device(
    layer_inputs, output_grads, input_basis, grad_basis, eigenvalues, layer_table, batch_ids
):
    parts = layer_parts(
        layer_inputs[0], output_grads[0], input_basis[0], grad_basis[0, 0], eigenvalues[0]
    )
    layer_scores = jnp.swapaxes(parts[:, :, :NQ], 1, 2)
    scores = jnp.sum(layer_scores, axis=0)
    batch_marks = (batch_ids[:, None] == jnp.arange(NB, dtype=jnp.int32)[None, :]).astype(F32)
    batch_scores = jnp.sum(scores[:, :, None] * batch_marks[None, :, :], axis=1)
    layer_marks = (layer_table[:, None] == jnp.arange(LAYERS, dtype=jnp.int32)[None, :]).astype(F32)
    layer_sums = jnp.sum(layer_scores, axis=2)
    layer_totals = jnp.sum(layer_marks[:, :, None] * layer_sums[:, None, :], axis=0)
    return (scores, batch_scores, layer_totals)


def solution(mesh):
    in_specs = (
        P("layer", "shard", None),
        P("layer", "shard", None),
        P("layer", None, None, None),
        P("layer", "shard", None, None),
        P("layer", "shard", None),
        P(),
        P(),
    )
    out_specs = (P(), P(), P())
    return jax.shard_map(
        per_device, mesh=mesh, in_specs=in_specs, out_specs=out_specs, check_vma=False
    )
```

time: 796 us -> 161 us (0.20); the launches traced: 785 us -> 161 us
  matrix products: 452 us -> 0 us
  Pallas kernels: 0 us -> 158 us
  local copies, waits for them, and re-layouts: 128 us -> 0.08 us
  other arithmetic: 98.7 us -> 2.19 us
  blocking collectives: 66.5 us -> 0 us
  waiting for transfers between devices: 14.1 us -> 0 us
  between operations: 14.4 us -> 0.66 us
  starting transfers between devices: 11.7 us -> 0 us
    dot_general x14 -> x0, matrix products: 452 us -> none  [the longest x4 334 us: per_device(): jnp.einsum('qij,tij->qt', weighted, train_grad, preferred_element_type=jn...]
    pallas_call x0 -> x1, Pallas kernels: none -> 158 us  [layer_parts(): pl.pallas_call(kernel, out_shape=jax.ShapeDtypeStruct((LAYERS, NT, 128),...]
    unnamed x1 -> x0, other arithmetic: 90.9 us -> none
    unnamed x22 -> x7, local copies, waits for them, and re-layouts: 70.6 us -> 0.08 us
    psum x1 -> x0, blocking collectives: 66.5 us -> none  [per_device(): lax.psum((partial_value, totals_part), ('layer', 'shard'))]
    all_gather x1 -> x0, local copies, waits for them, and re-layouts: 20.6 us -> none  [per_device(): lax.all_gather(layer_inputs, 'shard', axis=1, tiled=True)]
    slice x5 -> x0, local copies, waits for them, and re-layouts: 18.8 us -> none  [the longest x1 9.16 us: per_device(): train_in = input_proj[0, query_rows:].reshape(NT, ST, model_width)]
    all_to_all x3 -> x0, local copies, waits for them, and re-layouts: 17.5 us -> none  [per_device(): lax.all_to_all(output_grads, 'shard', split_axis=2, concat_axis=1, tiled=...]
  transfers between devices with their start and end apart: 2 -> 0, of which waited for: 1 -> 0; matrix products, arithmetic and copies ran while one was open for 22% -> 0% of each run, Pallas kernels for 0% -> 0%
where the time goes in v1:
time: 161 us
  Pallas kernels  158 us (98%)
  other arithmetic  2.19 us (1%)
    pallas_call x1, Pallas kernels, layer_parts(): pl.pallas_call(kernel, out_shape=jax.ShapeDtypeStruct((LAYERS, NT, 128),...  158 us

profile of v1, /device:TPU:1, one launch (start us, length us, event | category | flops | bytes accessed | tf_op | source)
XLA Modules:
  0.0 161.2 jit_solution(17812030852847837334)
XLA Ops:
  0.6 0.0 copy-start.1
  0.6 0.0 copy-start.2
  0.7 158.2 %shard_map.94 = f32[4,16,128]{2,1,0:T(8,128)} custom-call(bf16[48,5120]{1,0:T(8,128)(2,1)} %bitcast.10, bf16[48,16384]{1,0:T(8,128)(2,1)} %bitcast.8, bf16[10,512,512]{2,1,0:T(8,128)(2,1)} %bitcast.7, bf16[512,512]{1,0:T(8,128)(2,1)} %bitcast.9, f32[512,5120]{1,0:T(8,128)} %bitcast.6), custom_call_target="tpu_custom_call" | custom-call | tf_op jit(solution)/shard_map/pallas_call | solution.py:349
  158.9 0.8 slice_reduce_fusion
  159.7 0.1 copy.13
  159.7 0.0 copy-done.1
  159.7 0.0 copy-start
  159.7 0.7 multiply_reduce_fusion
  160.4 0.0 copy-done.2
  160.4 0.1 fusion.1
  160.5 0.7 multiply_reduce_fusion.1
  161.1 0.0 copy-done
  (1 shorter events, 0.0 us)
Async XLA Ops:
  0.6 159.1 %copy-start.1 = (s32[16]{0:T(128)S(1)}, s32[16]{0:T(128)}, u32[]{:S(2)}) copy-start(s32[16]{0:T(128)} %param.13) | copy-start | bytes 196
  0.6 159.8 %copy-start.2 = (s32[4]{0:T(128)S(1)}, s32[4]{0:T(128)}, u32[]{:S(2)}) copy-start(s32[4]{0:T(128)} %param.12) | copy-start | bytes 52
  159.7 1.4 copy-start
